TPU v7x, 128 devices: a whole 4x4x4 slice. The times are simulated.
128 devices in a mesh: seq: 32 (over x, z, core), head: 4 (over y).
Axes of the slice: x: 4, y: 4, z: 4, core: 2. Of those that a mesh axis runs over, the one named last changes fastest.
Arguments:
- tokens: bfloat16 [16384, 4096], P('seq', 'head'), may hold values from -80 to 80, as said below
- w_query: bfloat16 [4096, 2048], P(None, 'head'), may hold values from -0.09375 to 0.09375
- w_key: bfloat16 [4096, 2048], P(None, 'head'), may hold values from -0.09375 to 0.09375
- w_value: bfloat16 [4096, 2048], P(None, 'head'), may hold values from -0.09375 to 0.09375
- w_out: bfloat16 [2048, 4096], P('head'), may hold values from -0.125 to 0.125
- block_bucket: int32 [128], P('seq'), may hold values from 0 to 575, as said below
Outputs:
- attended: bfloat16 [16384, 4096], P('seq', 'head')
Inputs may be any that keep to these rules, and one draw needn't show every extreme that they name: `tokens`: hidden states of order one; a few rows may be far larger. `block_bucket`: no bucket holds more than 2 blocks, and some bucket holds exactly 2; an owner's buckets are numbered from its first id on and hold 2 blocks each except possibly its first and its last. The blocks of one index of seq belong to buckets of at most 1 block per owner, and some owner receives exactly 1 from every index of seq.
All inputs are finite; a program needn't handle non-finite values.
Results may differ from a plain program's by a relative error of at most 0.012.
The roundings to bfloat16 on the way count: a program that leaves them out, or rounds other values in their place, can miss the bound.
Values may be sent and summed in bfloat16 or wider, within the bound.
A program may use at most 128 MiB of HBM per device.

v0:
```python
import jax
import jax.numpy as jnp
from jax import lax
from jax.sharding import PartitionSpec as P

HDIM = 128
BMAX = 2


def in_blocks(array, dim, count):
    before, after = (array.shape[:dim], array.shape[dim + 1 :])
    return jnp.moveaxis(array.reshape(*before, count, -1, *after), dim, 0)


def piece_ends(length, count):
    turn = length // count
    if turn >= 8:
        turn -= turn % 8
    return [turn * k for k in range(1, count)]


def laid_out(blocks, dim):
    blocks = jnp.moveaxis(blocks, 0, dim)
    shape = blocks.shape
    return blocks.reshape(*shape[:dim], shape[dim] * shape[dim + 1], *shape[dim + 2 :])


def exchange_in_pieces(array, axis, pieces, split_dim, concat_dim):
    blocks = in_blocks(array, split_dim, lax.axis_size(axis))
    cut = max(range(1, max(2, blocks.ndim - 1)), key=lambda d: blocks.shape[d])
    finished = []
    for share in jnp.split(blocks, piece_ends(blocks.shape[cut], pieces), axis=cut):
        if share.size:
            finished.append(lax.all_to_all(share, axis, split_axis=0, concat_axis=0, tiled=True))
    return laid_out(jnp.concatenate(finished, axis=cut), concat_dim)


def key_lists(bucket, valid):
    count = bucket.shape[0]
    match = (bucket[:, None] == bucket[None, :]) & valid[None, :]
    rank = jnp.cumsum(match.astype(jnp.int32), axis=1) - 1
    picks = match[:, :, None] & (
        rank[:, :, None] == jnp.arange(BMAX, dtype=jnp.int32)[None, None, :]
    )
    places = jnp.arange(count, dtype=jnp.int32)[None, :, None]
    index = jnp.sum(jnp.where(picks, places, 0), axis=1)
    usable = jnp.any(picks, axis=1)
    return (index, usable)


def per_device(tokens, w_query, w_key, w_value, w_out, block_bucket):
    seq_count = lax.axis_size("seq")
    head_count = lax.axis_size("head")
    blocks_here = block_bucket.shape[0]
    tok_here = tokens.shape[0]
    block_len = tok_here // blocks_here
    capacity = (blocks_here + seq_count - 1) // seq_count
    slot_count = seq_count * capacity
    local_width = w_query.shape[1]
    heads_here = local_width // HDIM
    owned = seq_count * capacity // BMAX + 2
    piece = lax.all_gather(tokens, "head", axis=1, tiled=True)
    query, keys, values = tuple(
        (
            jnp.dot(piece, weight, preferred_element_type=jnp.float32)
            for weight in (w_query, w_key, w_value)
        )
    )
    packed = jnp.concatenate(
        [query.astype(jnp.bfloat16), keys.astype(jnp.bfloat16), values.astype(jnp.bfloat16)], axis=1
    )
    packed = packed.reshape(blocks_here, block_len, 3 * local_width)
    owner = block_bucket // owned
    places = jnp.arange(blocks_here, dtype=jnp.int32)
    earlier = (owner[:, None] == owner[None, :]) & (places[None, :] < places[:, None])
    rank = jnp.sum(earlier.astype(jnp.int32), axis=1)
    slot_of_block = owner * capacity + rank
    hits = slot_of_block[None, :] == jnp.arange(slot_count, dtype=jnp.int32)[:, None]
    source_index = jnp.sum(jnp.where(hits, places[None, :], 0), axis=1)
    filled = jnp.any(hits, axis=1)
    outgoing = jnp.take(packed, source_index, axis=0)
    outgoing_ids = jnp.where(filled, jnp.take(block_bucket, source_index), -1)
    arrived, arrived_ids = (
        exchange_in_pieces(outgoing, "seq", 2, 0, 0),
        exchange_in_pieces(outgoing_ids, "seq", 2, 0, 0),
    )
    index, usable = key_lists(arrived_ids, arrived_ids >= 0)
    mask = jnp.repeat(usable, block_len, axis=1)

    def head_attend(which):
        query_head = lax.dynamic_slice_in_dim(arrived, which * HDIM, HDIM, 2)
        key_head = lax.dynamic_slice_in_dim(arrived, local_width + which * HDIM, HDIM, 2)
        value_head = lax.dynamic_slice_in_dim(arrived, 2 * local_width + which * HDIM, HDIM, 2)
        key_rows = jnp.take(key_head, index, axis=0).reshape(slot_count, BMAX * block_len, HDIM)
        value_rows = jnp.take(value_head, index, axis=0).reshape(slot_count, BMAX * block_len, HDIM)
        scores = jnp.einsum(
            "sqd,skd->sqk", query_head, key_rows, preferred_element_type=jnp.float32
        ) * HDIM ** (-0.5)
        scores = jnp.where(mask[:, None, :], scores, -1e30)
        top = jnp.max(scores, axis=-1, keepdims=True)
        expo = jnp.exp(scores - top)
        weights = (expo / jnp.sum(expo, axis=-1, keepdims=True)).astype(jnp.bfloat16)
        mixed = jnp.einsum("sqk,skd->sqd", weights, value_rows, preferred_element_type=jnp.float32)
        return mixed.astype(jnp.bfloat16)

    per_head = lax.map(head_attend, jnp.arange(heads_here, dtype=jnp.int32))
    results = jnp.transpose(per_head, (1, 2, 0, 3)).reshape(slot_count, block_len, local_width)
    returned = lax.all_to_all(results, "seq", split_axis=0, concat_axis=0, tiled=True)
    mixed_here = jnp.take(returned, slot_of_block, axis=0).reshape(tok_here, local_width)
    column_width = w_out.shape[1] // head_count
    rows_split = w_out.reshape(local_width, head_count, column_width)
    columns = lax.all_to_all(rows_split, "head", split_axis=1, concat_axis=0, tiled=True)
    columns = columns.reshape(head_count * local_width, column_width)
    summed = jnp.dot(
        lax.all_gather(mixed_here, "head", axis=1, tiled=True),
        columns,
        preferred_element_type=jnp.float32,
    )
    return summed.astype(jnp.bfloat16)


def solution(mesh):
    placed = (
        P("seq", "head"),
        P(None, "head"),
        P(None, "head"),
        P(None, "head"),
        P("head", None),
        P("seq"),
    )
    return jax.shard_map(
        per_device, mesh=mesh, in_specs=placed, out_specs=P("seq", "head"), check_vma=False
    )
```

profile of v0, /device:TPU:0, one launch (start us, length us, event | category | flops | bytes accessed | tf_op | source)
XLA Modules:
  0.0 513.7 jit_solution(11713508505914483083)
XLA Ops:
  13.6 8.2 %all-to-all-start = ((s32[32,1,1]{2,1,0:T(1,128)}), s32[32,1,1]{2,1,0:T(1,128)S(1)}, u32[]{:S(2)}, u32[]{:S(2)}) async-start(s32[32,1,1]{2,1,0:T(1,128)} %copy.33), calls=%async_computation | async-start | bytes 32768 | tf_op jit(solution)/shard_map/all_to_all | solution.py:34
  21.9 37.8 %all-gather.3.cloned.1.call-done = bf16[512,4096]{1,0:T(8,128)(2,1)} async-done(((bf16[512,1024]{1,0:T(8,128)(2,1)}), bf16[512,4096]{1,0:T(8,128)(2,1)}) %all-gather.3.cloned.1.call-update) | async-done | bytes 4194320 | tf_op jit(solution)/shard_map/all_gather | solution.py:62
  59.8 6.0 %convolution_convert_fusion.1 = bf16[512,512]{0,1:T(8,128)(2,1)S(1)} fusion(bf16[512,4096]{1,0:T(8,128)(2,1)} %all-gather.3.cloned.1.call-done, bf16[4096,512]{1,0:T(8,128)(2,1)} %param.13), kind=kOutput, calls=%fused_computation.36 | convolution fusion | flops 2147745792 | bytes 8912896 | tf_op jit(solution)/shard_map/dot_general | solution.py:65
  71.4 6.4 %gather_fusion.2 = bf16[32,128,1536]{2,1,0:T(8,128)(2,1)} fusion(bf16[4,128,1536]{2,1,0:T(8,128)(2,1)S(1)} %bitcast.85, s32[1024]{0:T(1024)S(1)} %pad_clamp_fusion.2), kind=kCustom, calls=%fused_computation.2 | custom fusion | bytes 25165952 | tf_op jit(solution)/shard_map/jit(_take)/gather | solution.py:81
  77.8 6.5 %bitcast_select_fusion = bf16[32,1,128,1536]{3,2,0,1:T(8,128)(2,1)S(1)} fusion(bf16[32,128,1536]{2,1,0:T(8,128)(2,1)} %gather_fusion.2, pred[32]{0:T(512)(128)(4,1)S(1)} %compare_and_fusion.2), kind=kLoop, calls=%fused_computation.31 | loop fusion | flops 6291456 | bytes 25165856 | tf_op jit(solution)/shard_map/jit(_take)/select_n | solution.py:81
  84.3 4.9 slice_bitcast_fusion.1
  89.3 80.4 %all_to_all.36 = bf16[32,1,64,1536]{3,2,1,0:T(8,128)(2,1)} all-to-all(bf16[32,1,64,1536]{3,2,1,0:T(8,128)(2,1)} %get-tuple-element.126), channel_id=1, replica_groups=mesh['seq'=32,'head'=4] {'seq'}, dimensions={0} | all-to-all | bytes 12582912 | tf_op jit(solution)/shard_map/all_to_all | solution.py:34
  169.6 5.1 all-to-all-start.2
  176.1 78.4 %all-to-all-done.2 = bf16[32,1,64,1536]{3,2,1,0:T(8,128)(2,1)} async-done(((bf16[32,1,64,1536]{3,2,1,0:T(8,128)(2,1)}), bf16[32,1,64,1536]{3,2,1,0:T(8,128)(2,1)}, u32[]{:S(2)}, u32[]{:S(2)}) %all-to-all-start.2) | async-done | bytes 6291488 | tf_op jit(solution)/shard_map/all_to_all | solution.py:34
  254.5 10.6 %maximum_bitcast_fusion = bf16[32,128,1536]{2,1,0:T(8,128)(2,1)} fusion(bf16[32,1,64,1536]{3,2,1,0:T(8,128)(2,1)} %all-to-all-done.2, bf16[32,1,64,1536]{3,2,1,0:T(8,128)(2,1)} %all_to_all.36), kind=kLoop, calls=%fused_computation.30 | loop fusion | flops 25165824 | bytes 25165824 | tf_op jit(solution)/shard_map/reshape | solution.py:25
  265.1 94.5 %while.13 = (s32[]{:T(128)}, bf16[4,32,128,128]{2,3,0,1:T(8,128)(2,1)}, s32[4]{0:T(128)S(1)}, bf16[32,128,1536]{2,1,0:T(8,128)(2,1)}, s32[32,2]{1,0:T(8,128)S(1)...) while((s32[]{:T(128)}, ...), condition=%wide.region_9.11_spmd.clone, body=%wide.region_6.10_spmd.clone.sunk | while | flops 547882816 | bytes 65084444 | solution.py:106
  279.3 6.5 %fusion.44 = (f32[32,128]{1,0:T(8,128)S(1)}, f32[32,128,256]{2,1,0:T(8,128)S(1)}) fusion(f32[32,128,256]{2,1,0:T(8,128)S(1)} %fusion.43, pred[32,256]{1,0:T(8,128)(4,1)S(1)} %bitcast.91), kind=kOutput, calls=%fused_computation.71.clone.1 | output fusion | flops 6291711 | bytes 8413184 | tf_op jit(solution)/shard_map/while/body/eval_jaxpr/sub | solution.py:101
  302.9 6.5 %fusion.44 = (f32[32,128]{1,0:T(8,128)S(1)}, f32[32,128,256]{2,1,0:T(8,128)S(1)}) fusion(f32[32,128,256]{2,1,0:T(8,128)S(1)} %fusion.43, pred[32,256]{1,0:T(8,128)(4,1)S(1)} %bitcast.91), kind=kOutput, calls=%fused_computation.71.clone.1 | output fusion | flops 6291711 | bytes 8413184 | tf_op jit(solution)/shard_map/while/body/eval_jaxpr/sub | solution.py:101
  319.8 4.0 broadcast_select_fusion.3
  326.6 6.5 %fusion.44 = (f32[32,128]{1,0:T(8,128)S(1)}, f32[32,128,256]{2,1,0:T(8,128)S(1)}) fusion(f32[32,128,256]{2,1,0:T(8,128)S(1)} %fusion.43, pred[32,256]{1,0:T(8,128)(4,1)S(1)} %bitcast.91), kind=kOutput, calls=%fused_computation.71.clone.1 | output fusion | flops 6291711 | bytes 8413184 | tf_op jit(solution)/shard_map/while/body/eval_jaxpr/sub | solution.py:101
  343.4 4.0 broadcast_select_fusion.3
  350.2 6.5 %fusion.44 = (f32[32,128]{1,0:T(8,128)S(1)}, f32[32,128,256]{2,1,0:T(8,128)S(1)}) fusion(f32[32,128,256]{2,1,0:T(8,128)S(1)} %fusion.43, pred[32,256]{1,0:T(8,128)(4,1)S(1)} %bitcast.91), kind=kOutput, calls=%fused_computation.71.clone.1 | output fusion | flops 6291711 | bytes 8413184 | tf_op jit(solution)/shard_map/while/body/eval_jaxpr/sub | solution.py:101
  359.7 11.3 %all-to-all-start.3 = ((bf16[32,128,512]{1,2,0:T(8,128)(2,1)}), bf16[32,128,512]{1,2,0:T(8,128)(2,1)}, u32[]{:S(2)}, u32[]{:S(2)}) async-start(bf16[32,128,512]{1,2,0:T(8,128)(2,1)} %bitcast.88), calls=%async_computation.3 | async-start | bytes 8388608 | tf_op jit(solution)/shard_map/all_to_all | solution.py:108
  370.9 6.5 %copy.38 = bf16[512,4096]{0,1:T(8,128)(2,1)} copy(bf16[512,4096]{1,0:T(8,128)(2,1)} %param.14) | data formatting | bytes 8388608 | tf_op args[4]
  377.6 46.1 %all-to-all-done.3 = bf16[32,128,512]{1,2,0:T(8,128)(2,1)} async-done(((bf16[32,128,512]{1,2,0:T(8,128)(2,1)}), bf16[32,128,512]{1,2,0:T(8,128)(2,1)}, u32[]{:S(2)}, u32[]{:S(2)}) %all-to-all-start.3) | async-done | bytes 4194336 | tf_op jit(solution)/shard_map/all_to_all | solution.py:108
  423.7 4.9 all-to-all-start.4
  432.6 61.8 %all-to-all-done.4 = bf16[512,4,1024]{0,2,1:T(8,128)(2,1)} async-done(((bf16[512,4,1024]{0,2,1:T(8,128)(2,1)}), bf16[512,4,1024]{0,2,1:T(8,128)(2,1)}, u32[]{:S(2)}, u32[]{:S(2)}) %all-to-all-start.4) | async-done | bytes 4194336 | tf_op jit(solution)/shard_map/all_to_all | solution.py:112
  494.4 6.3 %copy.39 = bf16[4,512,1,1024]{3,1,0,2:T(8,128)(2,1)} copy(bf16[4,512,1,1024]{1,3,0,2:T(8,128)(2,1)} %bitcast.20) | data formatting | bytes 8388608 | tf_op jit(solution)/shard_map/all_to_all | solution.py:112
  500.7 6.1 %convolution_convert_fusion = bf16[512,1024]{1,0:T(8,128)(2,1)} fusion(bf16[512,2048]{1,0:T(8,128)(2,1)} %all-gather.5.cloned.1.call-done, bf16[2048,1024]{1,0:T(8,128)(2,1)} %bitcast.89), kind=kOutput, calls=%fused_computation.35 | convolution fusion | flops 2148007936 | bytes 7340032 | tf_op jit(solution)/shard_map/dot_general | solution.py:114
  (118 shorter events, 75.9 us)
Async XLA Ops:
  6.5 53.2 %all-gather.3.cloned.1.call-start = ((), (), s32[]{:S(2)}) async-start(), calls=%async_computation.5 | async-start | bytes 5242880 | tf_op jit(solution)/shard_map/all_gather | solution.py:62
  13.6 75.6 %all-to-all-start = ((s32[32,1,1]{2,1,0:T(1,128)}), s32[32,1,1]{2,1,0:T(1,128)S(1)}, u32[]{:S(2)}, u32[]{:S(2)}) async-start(s32[32,1,1]{2,1,0:T(1,128)} %copy.33), calls=%async_computation | async-start | bytes 32768 | tf_op jit(solution)/shard_map/all_to_all | solution.py:34
  59.8 6.0 %copy-start.2 = (bf16[4096,512]{1,0:T(8,128)(2,1)S(1)}, bf16[4096,512]{1,0:T(8,128)(2,1)}, u32[]{:S(2)}) copy-start(bf16[4096,512]{1,0:T(8,128)(2,1)} %param.12) | copy-start | bytes 12582916
  59.8 6.0 %copy-start.4 = (bf16[512,4096]{1,0:T(8,128)(2,1)S(1)}, bf16[512,4096]{1,0:T(8,128)(2,1)}, u32[]{:S(2)}) copy-start(bf16[512,4096]{1,0:T(8,128)(2,1)} %all-gather.3.cloned.1.call-done) | copy-start | bytes 12582916
  65.8 2.4 copy-start.3
  169.6 84.9 %all-to-all-start.2 = ((bf16[32,1,64,1536]{3,2,1,0:T(8,128)(2,1)}), bf16[32,1,64,1536]{3,2,1,0:T(8,128)(2,1)}, u32[]{:S(2)}, u32[]{:S(2)}) async-start(bf16[32,1,64,1536]{3,2,1,0:T(8,128)(2,1)} %get-tuple-element.127), calls=%async_computation.2 | async-start | bytes 12582912 | tf_op jit(solution)/shard_map/all_to_all | solution.py:34
  270.3 2.2 copy-start
  279.3 6.5 %copy-start.1 = (bf16[32,2,128,128]{3,2,1,0:T(8,128)(2,1)S(1)}, bf16[32,2,128,128]{3,2,1,0:T(8,128)(2,1)}, u32[]{:S(2)}) copy-start(bf16[32,2,128,128]{3,2,1,0:T(8,128)(2,1)} %get-tuple-element.179) | copy-start | bytes 6291460 | tf_op jit(solution)/shard_map/while
  294.0 2.2 copy-start
  302.9 6.5 %copy-start.1 = (bf16[32,2,128,128]{3,2,1,0:T(8,128)(2,1)S(1)}, bf16[32,2,128,128]{3,2,1,0:T(8,128)(2,1)}, u32[]{:S(2)}) copy-start(bf16[32,2,128,128]{3,2,1,0:T(8,128)(2,1)} %get-tuple-element.179) | copy-start | bytes 6291460 | tf_op jit(solution)/shard_map/while
  317.6 2.2 copy-start
  326.6 6.5 %copy-start.1 = (bf16[32,2,128,128]{3,2,1,0:T(8,128)(2,1)S(1)}, bf16[32,2,128,128]{3,2,1,0:T(8,128)(2,1)}, u32[]{:S(2)}) copy-start(bf16[32,2,128,128]{3,2,1,0:T(8,128)(2,1)} %get-tuple-element.179) | copy-start | bytes 6291460 | tf_op jit(solution)/shard_map/while
  341.2 2.2 copy-start
  350.2 6.5 %copy-start.1 = (bf16[32,2,128,128]{3,2,1,0:T(8,128)(2,1)S(1)}, bf16[32,2,128,128]{3,2,1,0:T(8,128)(2,1)}, u32[]{:S(2)}) copy-start(bf16[32,2,128,128]{3,2,1,0:T(8,128)(2,1)} %get-tuple-element.179) | copy-start | bytes 6291460 | tf_op jit(solution)/shard_map/while
  359.7 64.0 %all-to-all-start.3 = ((bf16[32,128,512]{1,2,0:T(8,128)(2,1)}), bf16[32,128,512]{1,2,0:T(8,128)(2,1)}, u32[]{:S(2)}, u32[]{:S(2)}) async-start(bf16[32,128,512]{1,2,0:T(8,128)(2,1)} %bitcast.88), calls=%async_computation.3 | async-start | bytes 8388608 | tf_op jit(solution)/shard_map/all_to_all | solution.py:108
  423.7 70.7 %all-to-all-start.4 = ((bf16[512,4,1024]{0,2,1:T(8,128)(2,1)}), bf16[512,4,1024]{0,2,1:T(8,128)(2,1)}, u32[]{:S(2)}, u32[]{:S(2)}) async-start(bf16[512,4,1024]{0,2,1:T(8,128)(2,1)} %bitcast.87), calls=%async_computation.4 | async-start | bytes 8388608 | tf_op jit(solution)/shard_map/all_to_all | solution.py:112
  428.5 72.2 %all-gather.5.cloned.1.call-start = ((), (), s32[]{:S(2)}) async-start(), calls=%async_computation.6 | async-start | bytes 2621440 | tf_op jit(solution)/shard_map/all_gather | solution.py:115
Sparse Core Ops, SparseCore 0:
  9.0 50.6 all-gather.2
  432.7 48.4 all-gather.4
where the time goes:
time: 515 us; the launch traced here: 514 us
  waiting for transfers between devices  225 us (44%)
  blocking collectives  80.4 us (16%)
  other arithmetic  65.6 us (13%)
  local copies, waits for them, and re-layouts  65.2 us (13%)
  matrix products  31.7 us (6%)
  starting transfers between devices  29.5 us (6%)
  between operations  13.6 us (3%)
    all_to_all x1, blocking collectives, exchange_in_pieces(): lax.all_to_all(share, axis, split_axis=0, concat_axis=0, tiled=True)  80.4 us
    all_to_all x2, waiting for transfers between devices, exchange_in_pieces(): lax.all_to_all(share, axis, split_axis=0, concat_axis=0, tiled=True)  78.4 us
    all_to_all x1, waiting for transfers between devices, per_device(): lax.all_to_all(rows_split, 'head', split_axis=1, concat_axis=0, tiled=True)  61.8 us
    all_to_all x1, waiting for transfers between devices, per_device(): lax.all_to_all(results, 'seq', split_axis=0, concat_axis=0, tiled=True)  46.1 us
    all_gather x1, waiting for transfers between devices, per_device(): piece = lax.all_gather(tokens, 'head', axis=1, tiled=True)  37.8 us
    sub x4, other arithmetic, head_attend(): expo = jnp.exp(scores - top)  25.9 us
    select_n x8, other arithmetic, head_attend(): jnp.take(key_head, index, axis=0)  16 us
    all_to_all x2, starting transfers between devices, exchange_in_pieces(): lax.all_to_all(share, axis, split_axis=0, concat_axis=0, tiled=True)  13.3 us
  transfers between devices with their start and end apart: 6, of which 4 were waited for; matrix products, arithmetic and copies ran while one was open for 11% of the time, Pallas kernels for 0%

commit v1 on v0

--- a/solution.py
+++ b/solution.py
@@ -59,7 +59,9 @@
     local_width = w_query.shape[1]
     heads_here = local_width // HDIM
     owned = seq_count * capacity // BMAX + 2
-    piece = lax.all_gather(tokens, "head", axis=1, tiled=True)
+    piece = jnp.concatenate(
+        lax.all_to_all(jnp.stack([tokens] * lax.axis_size("head")), "head", 0, 0), axis=1
+    )
     query, keys, values = tuple(
         (
             jnp.dot(piece, weight, preferred_element_type=jnp.float32)

time: 515 us -> 533 us (1.035)
  waiting for transfers between devices: 225 us -> 231 us
    all_to_all x0 -> x1, waiting for transfers between devices: none -> 45 us  [per_device(): lax.all_to_all(jnp.stack([tokens] * lax.axis_size('head')), 'head', 0, 0)]
    all_gather x1 -> x0, waiting for transfers between devices: 37.8 us -> none  [per_device(): piece = lax.all_gather(tokens, 'head', axis=1, tiled=True)]
where the time goes in v1:
time: 533 us; the launch traced here: 531 us
  waiting for transfers between devices  231 us (43%)
  blocking collectives  80.5 us (15%)
  local copies, waits for them, and re-layouts  68.1 us (13%)
  other arithmetic  64.3 us (12%)
  matrix products  36.3 us (7%)
  starting transfers between devices  34.5 us (6%)
  between operations  13.6 us (3%)
    all_to_all x1, blocking collectives, exchange_in_pieces(): lax.all_to_all(share, axis, split_axis=0, concat_axis=0, tiled=True)  80.5 us
    all_to_all x2, waiting for transfers between devices, exchange_in_pieces(): lax.all_to_all(share, axis, split_axis=0, concat_axis=0, tiled=True)  78.4 us
    all_to_all x1, waiting for transfers between devices, per_device(): lax.all_to_all(rows_split, 'head', split_axis=1, concat_axis=0, tiled=True)  61.8 us
    all_to_all x1, waiting for transfers between devices, per_device(): lax.all_to_all(results, 'seq', split_axis=0, concat_axis=0, tiled=True)  46.1 us
    all_to_all x1, waiting for transfers between devices, per_device(): lax.all_to_all(jnp.stack([tokens] * lax.axis_size('head')), 'head', 0, 0)  45 us
    sub x4, other arithmetic, head_attend(): expo = jnp.exp(scores - top)  25.9 us
    select_n x8, other arithmetic, head_attend(): jnp.take(key_head, index, axis=0)  16.1 us
    dot_general x3, matrix products, per_device(): jnp.dot(piece, weight, preferred_element_type=jnp.float32)  15.3 us
  transfers between devices with their start and end apart: 6, of which 4 were waited for; matrix products, arithmetic and copies ran while one was open for 11% of the time, Pallas kernels for 0%

profile of v1, /device:TPU:0, one launch (start us, length us, event | category | flops | bytes accessed | tf_op | source)
XLA Modules:
  0.0 531.3 jit_solution(6744115863212240218)
XLA Ops:
  10.3 5.0 all-to-all-start.1
  19.5 45.0 %all-to-all-done.1 = bf16[4,512,1024]{1,2,0:T(8,128)(2,1)} async-done(((bf16[4,512,1024]{1,2,0:T(8,128)(2,1)}), bf16[4,512,1024]{1,2,0:T(8,128)(2,1)}, u32[]{:S(2)}, u32[]{:S(2)}) %all-to-all-start.1) | async-done | bytes 4194336 | tf_op jit(solution)/shard_map/all_to_all | solution.py:63
  64.5 8.2 %all-to-all-start = ((s32[32,1,1]{2,1,0:T(1,128)}), s32[32,1,1]{2,1,0:T(1,128)S(1)}, u32[]{:S(2)}, u32[]{:S(2)}) async-start(s32[32,1,1]{2,1,0:T(1,128)} %copy.38), calls=%async_computation | async-start | bytes 32768 | tf_op jit(solution)/shard_map/all_to_all | solution.py:34
  72.7 6.0 %convolution_convert_fusion.1 = bf16[512,512]{0,1:T(8,128)(2,1)S(1)} fusion(bf16[512,4096]{0,1:T(8,128)(2,1)} %bitcast.2, bf16[4096,512]{1,0:T(8,128)(2,1)} %param.13), kind=kOutput, calls=%fused_computation.36 | convolution fusion | flops 2147745792 | bytes 8912896 | tf_op jit(solution)/shard_map/dot_general | solution.py:67
  78.7 4.8 convolution_convert_fusion.2
  88.9 6.4 %gather_fusion.2 = bf16[32,128,1536]{2,1,0:T(8,128)(2,1)} fusion(bf16[4,128,1536]{2,1,0:T(8,128)(2,1)S(1)} %bitcast.88, s32[1024]{0:T(1024)S(1)} %pad_clamp_fusion.2), kind=kCustom, calls=%fused_computation.2 | custom fusion | bytes 25165952 | tf_op jit(solution)/shard_map/jit(_take)/gather | solution.py:83
  95.4 6.5 %bitcast_select_fusion = bf16[32,1,128,1536]{3,2,0,1:T(8,128)(2,1)S(1)} fusion(bf16[32,128,1536]{2,1,0:T(8,128)(2,1)} %gather_fusion.2, pred[32]{0:T(512)(128)(4,1)S(1)} %compare_and_fusion.2), kind=kLoop, calls=%fused_computation.31 | loop fusion | flops 6291456 | bytes 25165856 | tf_op jit(solution)/shard_map/jit(_take)/select_n | solution.py:83
  101.9 4.9 slice_bitcast_fusion.1
  106.9 80.5 %all_to_all.41 = bf16[32,1,64,1536]{3,2,1,0:T(8,128)(2,1)} all-to-all(bf16[32,1,64,1536]{3,2,1,0:T(8,128)(2,1)} %get-tuple-element.126), channel_id=1, replica_groups=mesh['seq'=32,'head'=4] {'seq'}, dimensions={0} | all-to-all | bytes 12582912 | tf_op jit(solution)/shard_map/all_to_all | solution.py:34
  187.3 5.1 all-to-all-start.3
  193.8 78.4 %all-to-all-done.3 = bf16[32,1,64,1536]{3,2,1,0:T(8,128)(2,1)} async-done(((bf16[32,1,64,1536]{3,2,1,0:T(8,128)(2,1)}), bf16[32,1,64,1536]{3,2,1,0:T(8,128)(2,1)}, u32[]{:S(2)}, u32[]{:S(2)}) %all-to-all-start.3) | async-done | bytes 6291488 | tf_op jit(solution)/shard_map/all_to_all | solution.py:34
  272.2 10.6 %maximum_bitcast_fusion = bf16[32,128,1536]{2,1,0:T(8,128)(2,1)} fusion(bf16[32,1,64,1536]{3,2,1,0:T(8,128)(2,1)} %all-to-all-done.3, bf16[32,1,64,1536]{3,2,1,0:T(8,128)(2,1)} %all_to_all.41), kind=kLoop, calls=%fused_computation.30 | loop fusion | flops 25165824 | bytes 25165824 | tf_op jit(solution)/shard_map/reshape | solution.py:25
  282.8 94.5 %while.13 = (s32[]{:T(128)}, bf16[4,32,128,128]{2,3,0,1:T(8,128)(2,1)}, s32[4]{0:T(128)S(1)}, bf16[32,128,1536]{2,1,0:T(8,128)(2,1)}, s32[32,2]{1,0:T(8,128)S(1)...) while((s32[]{:T(128)}, ...), condition=%wide.region_9.11_spmd.clone, body=%wide.region_6.10_spmd.clone.sunk | while | flops 547882816 | bytes 65084444 | solution.py:108
  297.0 6.5 %fusion.44 = (f32[32,128]{1,0:T(8,128)S(1)}, f32[32,128,256]{2,1,0:T(8,128)S(1)}) fusion(f32[32,128,256]{2,1,0:T(8,128)S(1)} %fusion.43, pred[32,256]{1,0:T(8,128)(4,1)S(1)} %bitcast.94), kind=kOutput, calls=%fused_computation.71.clone.1 | output fusion | flops 6291711 | bytes 8413184 | tf_op jit(solution)/shard_map/while/body/eval_jaxpr/sub | solution.py:103
  320.7 6.5 %fusion.44 = (f32[32,128]{1,0:T(8,128)S(1)}, f32[32,128,256]{2,1,0:T(8,128)S(1)}) fusion(f32[32,128,256]{2,1,0:T(8,128)S(1)} %fusion.43, pred[32,256]{1,0:T(8,128)(4,1)S(1)} %bitcast.94), kind=kOutput, calls=%fused_computation.71.clone.1 | output fusion | flops 6291711 | bytes 8413184 | tf_op jit(solution)/shard_map/while/body/eval_jaxpr/sub | solution.py:103
  344.3 6.5 %fusion.44 = (f32[32,128]{1,0:T(8,128)S(1)}, f32[32,128,256]{2,1,0:T(8,128)S(1)}) fusion(f32[32,128,256]{2,1,0:T(8,128)S(1)} %fusion.43, pred[32,256]{1,0:T(8,128)(4,1)S(1)} %bitcast.94), kind=kOutput, calls=%fused_computation.71.clone.1 | output fusion | flops 6291711 | bytes 8413184 | tf_op jit(solution)/shard_map/while/body/eval_jaxpr/sub | solution.py:103
  367.9 6.5 %fusion.44 = (f32[32,128]{1,0:T(8,128)S(1)}, f32[32,128,256]{2,1,0:T(8,128)S(1)}) fusion(f32[32,128,256]{2,1,0:T(8,128)S(1)} %fusion.43, pred[32,256]{1,0:T(8,128)(4,1)S(1)} %bitcast.94), kind=kOutput, calls=%fused_computation.71.clone.1 | output fusion | flops 6291711 | bytes 8413184 | tf_op jit(solution)/shard_map/while/body/eval_jaxpr/sub | solution.py:103
  377.4 11.3 %all-to-all-start.4 = ((bf16[32,128,512]{1,2,0:T(8,128)(2,1)}), bf16[32,128,512]{1,2,0:T(8,128)(2,1)}, u32[]{:S(2)}, u32[]{:S(2)}) async-start(bf16[32,128,512]{1,2,0:T(8,128)(2,1)} %bitcast.91), calls=%async_computation.4 | async-start | bytes 8388608 | tf_op jit(solution)/shard_map/all_to_all | solution.py:110
  388.6 6.6 %copy.43 = bf16[512,4096]{0,1:T(8,128)(2,1)} copy(bf16[512,4096]{1,0:T(8,128)(2,1)} %param.14) | data formatting | bytes 8388608 | tf_op args[4]
  395.3 46.1 %all-to-all-done.4 = bf16[32,128,512]{1,2,0:T(8,128)(2,1)} async-done(((bf16[32,128,512]{1,2,0:T(8,128)(2,1)}), bf16[32,128,512]{1,2,0:T(8,128)(2,1)}, u32[]{:S(2)}, u32[]{:S(2)}) %all-to-all-start.4) | async-done | bytes 4194336 | tf_op jit(solution)/shard_map/all_to_all | solution.py:110
  441.4 4.9 all-to-all-start.5
  450.3 61.8 %all-to-all-done.5 = bf16[512,4,1024]{0,2,1:T(8,128)(2,1)} async-done(((bf16[512,4,1024]{0,2,1:T(8,128)(2,1)}), bf16[512,4,1024]{0,2,1:T(8,128)(2,1)}, u32[]{:S(2)}, u32[]{:S(2)}) %all-to-all-start.5) | async-done | bytes 4194336 | tf_op jit(solution)/shard_map/all_to_all | solution.py:114
  512.0 6.3 %copy.44 = bf16[4,512,1,1024]{3,1,0,2:T(8,128)(2,1)} copy(bf16[4,512,1,1024]{1,3,0,2:T(8,128)(2,1)} %bitcast.23) | data formatting | bytes 8388608 | tf_op jit(solution)/shard_map/all_to_all | solution.py:114
  518.4 6.1 %convolution_convert_fusion = bf16[512,1024]{1,0:T(8,128)(2,1)} fusion(bf16[512,2048]{1,0:T(8,128)(2,1)} %all-gather.2.cloned.1.call-done, bf16[2048,1024]{1,0:T(8,128)(2,1)} %bitcast.92), kind=kOutput, calls=%fused_computation.35 | convolution fusion | flops 2148007936 | bytes 7340032 | tf_op jit(solution)/shard_map/dot_general | solution.py:116
  (119 shorter events, 84.6 us)
Async XLA Ops:
  10.3 5.0 copy-start.2
  10.3 54.2 %all-to-all-start.1 = ((bf16[4,512,1024]{1,2,0:T(8,128)(2,1)}), bf16[4,512,1024]{1,2,0:T(8,128)(2,1)}, u32[]{:S(2)}, u32[]{:S(2)}) async-start(bf16[4,512,1024]{1,2,0:T(8,128)(2,1)} %stack.2), calls=%async_computation.1 | async-start | bytes 8388608 | tf_op jit(solution)/shard_map/all_to_all | solution.py:63
  64.5 42.4 %all-to-all-start = ((s32[32,1,1]{2,1,0:T(1,128)}), s32[32,1,1]{2,1,0:T(1,128)S(1)}, u32[]{:S(2)}, u32[]{:S(2)}) async-start(s32[32,1,1]{2,1,0:T(1,128)} %copy.38), calls=%async_computation | async-start | bytes 32768 | tf_op jit(solution)/shard_map/all_to_all | solution.py:34
  72.7 6.0 %copy-start.3 = (bf16[4096,512]{1,0:T(8,128)(2,1)S(1)}, bf16[4096,512]{1,0:T(8,128)(2,1)}, u32[]{:S(2)}) copy-start(bf16[4096,512]{1,0:T(8,128)(2,1)} %param.12) | copy-start | bytes 12582916
  78.7 4.8 copy-start.4
  187.3 84.8 %all-to-all-start.3 = ((bf16[32,1,64,1536]{3,2,1,0:T(8,128)(2,1)}), bf16[32,1,64,1536]{3,2,1,0:T(8,128)(2,1)}, u32[]{:S(2)}, u32[]{:S(2)}) async-start(bf16[32,1,64,1536]{3,2,1,0:T(8,128)(2,1)} %get-tuple-element.127), calls=%async_computation.3 | async-start | bytes 12582912 | tf_op jit(solution)/shard_map/all_to_all | solution.py:34
  288.0 2.2 copy-start
  297.0 6.5 %copy-start.1 = (bf16[32,2,128,128]{3,2,1,0:T(8,128)(2,1)S(1)}, bf16[32,2,128,128]{3,2,1,0:T(8,128)(2,1)}, u32[]{:S(2)}) copy-start(bf16[32,2,128,128]{3,2,1,0:T(8,128)(2,1)} %get-tuple-element.179) | copy-start | bytes 6291460 | tf_op jit(solution)/shard_map/while
  311.7 2.2 copy-start
  320.7 6.5 %copy-start.1 = (bf16[32,2,128,128]{3,2,1,0:T(8,128)(2,1)S(1)}, bf16[32,2,128,128]{3,2,1,0:T(8,128)(2,1)}, u32[]{:S(2)}) copy-start(bf16[32,2,128,128]{3,2,1,0:T(8,128)(2,1)} %get-tuple-element.179) | copy-start | bytes 6291460 | tf_op jit(solution)/shard_map/while
  335.3 2.2 copy-start
  344.3 6.5 %copy-start.1 = (bf16[32,2,128,128]{3,2,1,0:T(8,128)(2,1)S(1)}, bf16[32,2,128,128]{3,2,1,0:T(8,128)(2,1)}, u32[]{:S(2)}) copy-start(bf16[32,2,128,128]{3,2,1,0:T(8,128)(2,1)} %get-tuple-element.179) | copy-start | bytes 6291460 | tf_op jit(solution)/shard_map/while
  358.9 2.2 copy-start
  367.9 6.5 %copy-start.1 = (bf16[32,2,128,128]{3,2,1,0:T(8,128)(2,1)S(1)}, bf16[32,2,128,128]{3,2,1,0:T(8,128)(2,1)}, u32[]{:S(2)}) copy-start(bf16[32,2,128,128]{3,2,1,0:T(8,128)(2,1)} %get-tuple-element.179) | copy-start | bytes 6291460 | tf_op jit(solution)/shard_map/while
  377.4 64.0 %all-to-all-start.4 = ((bf16[32,128,512]{1,2,0:T(8,128)(2,1)}), bf16[32,128,512]{1,2,0:T(8,128)(2,1)}, u32[]{:S(2)}, u32[]{:S(2)}) async-start(bf16[32,128,512]{1,2,0:T(8,128)(2,1)} %bitcast.91), calls=%async_computation.4 | async-start | bytes 8388608 | tf_op jit(solution)/shard_map/all_to_all | solution.py:110
  441.4 70.7 %all-to-all-start.5 = ((bf16[512,4,1024]{0,2,1:T(8,128)(2,1)}), bf16[512,4,1024]{0,2,1:T(8,128)(2,1)}, u32[]{:S(2)}, u32[]{:S(2)}) async-start(bf16[512,4,1024]{0,2,1:T(8,128)(2,1)} %bitcast.90), calls=%async_computation.5 | async-start | bytes 8388608 | tf_op jit(solution)/shard_map/all_to_all | solution.py:114
  446.2 72.1 %all-gather.2.cloned.1.call-start = ((), (), s32[]{:S(2)}) async-start(), calls=%async_computation.6 | async-start | bytes 2621440 | tf_op jit(solution)/shard_map/all_gather | solution.py:117
Sparse Core Ops, SparseCore 0:
  450.4 48.4 all-gather.1
